TPU v7x, 32 devices: a whole 2x2x4 slice. The times are simulated.
32 devices in a mesh: parts: 1, row: 4 (over z), col: 4 (over y, x), rep: 2 (over core).
Axes of the slice: x: 2, y: 2, z: 4, core: 2. Of those that a mesh axis runs over, the one named last changes fastest.
Arguments:
- feats: bfloat16 [4096, 128], P(('parts', 'row', 'col', 'rep')), may hold values from -6 to 6
- weight: bfloat16 [128, 256], replicated, may hold values from -0.5 to 0.5
- tile_vals: bfloat16 [2048, 128, 128], P(('parts', 'row', 'col', 'rep')), may hold values from -0.09375 to 0.09375
- tile_rows: int32 [2048], P(('parts', 'row', 'col', 'rep')), may hold values from 0 to 7
- tile_cols: int32 [2048], P(('parts', 'row', 'col', 'rep')), may hold values from 0 to 7
- tile_count: int32 [32], P(('parts', 'row', 'col', 'rep')), may hold values from 16 to 64, as said below
- relu_mask: int32 [4096, 256], P(('parts', 'row', 'col', 'rep')), may hold values 0 or 1
- cotangent: bfloat16 [4096, 256], P(('parts', 'row', 'col', 'rep')), may hold values from -6 to 6
Outputs:
- activated: bfloat16 [4096, 256], P(('parts', 'row', 'col', 'rep'))
- grad_w: float32 [128, 256], P('parts')
- grad_x: bfloat16 [4096, 128], P(('parts', 'row', 'col', 'rep'))
Inputs may be any that keep to these rules, and one draw needn't show every extreme that they name: `tile_rows`: row block of a slot within its device's destination list. `tile_cols`: column block of a slot within its device's source list. `tile_count`: live slots are the first ones of a device; the rest are ignored; in every draw some device has all 64 slots live.
All inputs are finite; a program needn't handle non-finite values. No bound on the sum of `relu_mask` on one device may be relied on, other than what follows from the above.
Results may differ from a plain program's by a relative error of at most 0.005.
Values may be sent and summed in bfloat16 or wider, within the bound.
A program may use at most 64 MiB of HBM per device.

v0:
```python
import jax
import jax.numpy as jnp
from jax import lax
from jax.sharding import PartitionSpec as P

FEAT = 128
BLOCK = 128


tiles_per_turn = 4


def run_tiles(locate, finish, step_fn, init):
    turns = (finish + tiles_per_turn - 1) // tiles_per_turn

    def turn(index, carry):
        slots = index * tiles_per_turn + jnp.arange(tiles_per_turn, dtype=jnp.int32)
        live = slots < finish
        values, rows_here, cols_here = locate(slots)
        return step_fn(carry, values, rows_here, cols_here, live)

    return lax.fori_loop(0, turns, turn, init)


def body(feats, weight, tile_vals, tile_rows, tile_cols, tile_count, relu_mask, cotangent):
    slot_total = tile_vals.shape[0]
    rep_count = lax.axis_size("rep")
    row_count = lax.axis_size("row")
    node_dev = feats.shape[0]
    row_blocks = node_dev * lax.axis_size("col") * rep_count // BLOCK
    own_count = tile_count[0]

    def locate(slots):
        place = jnp.minimum(slots, slot_total - 1)
        return (
            jnp.take(tile_vals, place, axis=0),
            jnp.take(tile_rows, place),
            jnp.take(tile_cols, place),
        )

    gathered = lax.all_gather(feats, ("row", "rep"), axis=0, tiled=True)
    source_blocks = gathered.reshape(-1, BLOCK, FEAT)
    col_blocks = source_blocks.shape[0]

    def forward_step(total, values, rows_here, cols_here, live):
        inputs = jnp.take(source_blocks, cols_here, axis=0)
        product = jnp.einsum("tij,tjf->tif", values, inputs, preferred_element_type=jnp.float32)
        product = product * live.astype(jnp.float32)[:, None, None]
        return total.at[rows_here].add(product)

    dest_part = run_tiles(
        locate, own_count, forward_step, jnp.zeros((row_blocks, BLOCK, FEAT), jnp.float32)
    )
    agg = lax.psum_scatter(
        dest_part.reshape(row_blocks * BLOCK, FEAT), ("col", "rep"), scatter_dimension=0, tiled=True
    )
    agg_b = agg.astype(jnp.bfloat16)
    keep = relu_mask.astype(jnp.float32)
    hidden = jnp.dot(agg_b, weight, preferred_element_type=jnp.float32)
    activated = (hidden * keep).astype(jnp.bfloat16)
    grad_h = (cotangent.astype(jnp.float32) * keep).astype(jnp.bfloat16)
    weight_term = lax.dot_general(
        agg_b, grad_h, (((0,), (0,)), ((), ())), preferred_element_type=jnp.float32
    )
    node_total = node_dev * row_count * lax.axis_size("col") * rep_count
    grad_w = lax.psum(weight_term, ("row", "col", "rep")) * float(node_total) ** (-0.5)
    back = lax.dot_general(
        grad_h, weight, (((1,), (1,)), ((), ())), preferred_element_type=jnp.float32
    ).astype(jnp.bfloat16)
    dest_blocks = lax.all_gather(back, ("col", "rep"), axis=0, tiled=True).reshape(
        row_blocks, BLOCK, FEAT
    )

    def backward_step(total, values, rows_here, cols_here, live):
        inputs = jnp.take(dest_blocks, rows_here, axis=0)
        product = jnp.einsum("tij,tif->tjf", values, inputs, preferred_element_type=jnp.float32)
        product = product * live.astype(jnp.float32)[:, None, None]
        return total.at[cols_here].add(product)

    source_part = run_tiles(
        locate, own_count, backward_step, jnp.zeros((col_blocks, BLOCK, FEAT), jnp.float32)
    )
    grad_acc = lax.psum_scatter(
        source_part.reshape(col_blocks * BLOCK, FEAT),
        ("row", "rep"),
        scatter_dimension=0,
        tiled=True,
    )
    return (activated, grad_w, grad_acc.astype(jnp.bfloat16))


def solution(mesh):
    placed = (
        P(("parts", "row", "col", "rep"), None),
        P(),
        P(("parts", "row", "col", "rep"), None, None),
        P(("parts", "row", "col", "rep")),
        P(("parts", "row", "col", "rep")),
        P(("parts", "row", "col", "rep")),
        P(("parts", "row", "col", "rep"), None),
        P(("parts", "row", "col", "rep"), None),
    )
    return jax.shard_map(
        body,
        mesh=mesh,
        in_specs=placed,
        out_specs=(
            P(("parts", "row", "col", "rep"), None),
            P("parts", None),
            P(("parts", "row", "col", "rep"), None),
        ),
        check_vma=False,
    )
```

profile of v0, /device:TPU:0, one launch (start us, length us, event | category | flops | bytes accessed | tf_op | source)
XLA Modules:
  0.0 314.0 jit_solution(7151522205817065213)
XLA Ops:
  8.7 16.1 %all_gather.6 = bf16[1024,128]{1,0:T(8,128)(2,1)S(1)} all-gather(bf16[128,128]{1,0:T(8,128)(2,1)} %param.18), channel_id=1, replica_groups=mesh['parts'=1,'row'=4,'col'=4,'rep'=2] {'row','rep'}, dimensions={0}, use_global_device_ids=true | all-gather | bytes 294912 | tf_op jit(solution)/shard_map/all_gather | solution.py:41
  24.9 49.8 %while.20 = (s32[]{:T(128)}, f32[8,128,128]{2,1,0:T(8,128)S(1)}, s32[]{:T(128)}, s32[64]{0:T(128)}, bf16[64,128,128]{2,1,0:T(8,128)(2,1)}, /*index=5*/s32[64]{0:...) while((s32[]{:T(128)}, f32[8,128,128]{2,1,0:T(8,128)S(1)}, s32[]{:T(128)}, ...), condition=%wide.region_2.0_spmd, body=%wide.region_0.5_spmd.sunk | while | flops 17041552 | bytes 1843637 | solution.py:22
  24.9 1.3 gather_fusion.1
  26.9 2.2 gather_fusion.3
  30.0 1.3 gather_fusion
  32.1 1.3 gather_fusion.1
  34.0 2.2 gather_fusion.3
  37.1 1.3 gather_fusion
  38.4 0.8 scatter_fusion
  39.2 1.3 gather_fusion.1
  41.1 2.2 gather_fusion.3
  44.2 1.3 gather_fusion
  46.3 1.3 gather_fusion.1
  48.2 2.2 gather_fusion.3
  51.3 1.3 gather_fusion
  53.4 1.3 gather_fusion.1
  55.3 2.2 gather_fusion.3
  58.4 1.3 gather_fusion
  59.7 0.8 scatter_fusion
  60.5 1.3 gather_fusion.1
  62.4 2.2 gather_fusion.3
  65.5 1.3 gather_fusion
  66.8 0.7 scatter_fusion
  67.6 1.3 gather_fusion.1
  69.5 2.2 gather_fusion.3
  72.6 1.3 gather_fusion
  74.7 0.8 copy-done.4
  75.7 73.1 %all_gather.7 = bf16[1024,128]{1,0:T(8,128)(2,1)S(1)} all-gather(bf16[128,128]{1,0:T(8,128)(2,1)S(1)} %convolution_convert_fusion), channel_id=1, replica_groups=mesh['parts'=1,'row'=4,'col'=4,'rep'=2] {'col','rep'}, dimensions={0}, use_global_device_ids=true | all-gather | bytes 294912 | tf_op jit(solution)/shard_map/all_gather | solution.py:70
  148.8 25.0 %reduce-scatter.3.cloned.1.call-done = f32[128,128]{1,0:T(8,128)} async-done(((f32[1024,128]{1,0:T(8,128)}), f32[128,128]{1,0:T(8,128)}) %reduce-scatter.3.cloned.1.call-update) | async-done | bytes 65552 | tf_op jit(solution)/shard_map/reduce_scatter | solution.py:54
  173.8 1.7 fusion.13
  175.6 41.0 %while.21 = (s32[]{:T(128)}, f32[8,128,128]{2,1,0:T(8,128)S(1)}, s32[]{:T(128)}, s32[64]{0:T(128)S(1)}, bf16[64,128,128]{2,1,0:T(8,128)(2,1)}, /*index=5*/s32[64...) while((s32[]{:T(128)}, f32[8,128,128]{2,1,0:T(8,128)S(1)}, s32[]{:T(128)}, ...), condition=%wide.region_7.11_spmd, body=%wide.region_5.10_spmd.sunk | while | flops 17041552 | bytes 1843637 | solution.py:22
  176.9 2.2 gather_fusion.7
  180.7 0.8 scatter_fusion.1
  182.8 2.2 gather_fusion.7
  188.7 2.2 gather_fusion.7
  192.5 0.8 scatter_fusion.1
  194.5 2.2 gather_fusion.7
  200.4 2.2 gather_fusion.7
  204.2 0.8 scatter_fusion.1
  206.2 2.2 gather_fusion.7
  210.0 0.8 scatter_fusion.1
  212.1 2.2 gather_fusion.7
  215.9 0.8 scatter_fusion.1
  216.7 0.8 copy-done.3
  217.5 0.8 fusion.12
  218.3 85.3 %all-reduce.2.cloned.1.call-done = f32[128,256]{1,0:T(8,128)} async-done(((f32[128,256]{1,0:T(8,128)}), f32[128,256]{1,0:T(8,128)}) %all-reduce.2.cloned.1.call-update) | async-done | bytes 131088 | tf_op jit(solution)/shard_map/psum | solution.py:66
  303.5 1.6 broadcast_multiply_fusion
  305.1 1.5 convert_element_type.41
  (156 shorter events, 35.5 us)
Async XLA Ops:
  8.0 67.5 %copy-start = (bf16[128,256]{1,0:T(8,128)(2,1)S(1)}, bf16[128,256]{1,0:T(8,128)(2,1)}, u32[]{:S(2)}) copy-start(bf16[128,256]{1,0:T(8,128)(2,1)} %param.19) | copy-start | bytes 196612
  8.0 165.8 %reduce-scatter.3.cloned.1.call-start = ((), (), s32[]{:S(2)}) async-start(), calls=%async_computation.2 | async-start | bytes 589824 | tf_op jit(solution)/shard_map/reduce_scatter | solution.py:54
  24.9 50.7 %copy-start.5 = (s32[128,256]{1,0:T(8,128)S(1)}, s32[128,256]{1,0:T(8,128)}, u32[]{:S(2)}) copy-start(s32[128,256]{1,0:T(8,128)} %param.24) | copy-start | bytes 393220
  24.9 50.7 %copy-start.7 = (bf16[128,256]{1,0:T(8,128)(2,1)S(1)}, bf16[128,256]{1,0:T(8,128)(2,1)}, u32[]{:S(2)}) copy-start(bf16[128,256]{1,0:T(8,128)(2,1)} %param.25) | copy-start | bytes 196612
  74.6 0.8 copy-start.4
  74.7 101.0 %copy-start.1 = (s32[64]{0:T(128)S(1)}, s32[64]{0:T(128)}, u32[]{:S(2)}) copy-start(s32[64]{0:T(128)} %get-tuple-element.307) | copy-start | bytes 772
  74.7 101.0 %copy-start.2 = (s32[64]{0:T(128)S(1)}, s32[64]{0:T(128)}, u32[]{:S(2)}) copy-start(s32[64]{0:T(128)} %get-tuple-element.308) | copy-start | bytes 772
  75.5 228.1 %all-reduce.2.cloned.1.call-start = ((), (), s32[]{:S(2)}) async-start(), calls=%async_computation.3 | async-start | bytes 262144 | tf_op jit(solution)/shard_map/psum | solution.py:66
  175.5 129.6 %reduce-scatter.5.cloned.1.call-start = ((), (), s32[]{:S(2)}) async-start(), calls=%async_computation.4 | async-start | bytes 589824 | tf_op jit(solution)/shard_map/reduce_scatter | solution.py:83
  175.6 41.9 %copy-start.6 = (f32[128,128]{1,0:T(8,128)S(1)}, f32[128,128]{1,0:T(8,128)}, u32[]{:S(2)}) copy-start(f32[128,128]{1,0:T(8,128)} %reduce-scatter.3.cloned.1.call-done) | copy-start | bytes 196612
  216.7 0.8 copy-start.3
Sparse Core Ops, SparseCore 0:
  75.6 98.1 reduce-scatter.2
  180.8 122.6 all-reduce.1
Sparse Core Ops, SparseCore 1:
  217.6 83.6 reduce-scatter.4
where the time goes:
time: 315 us; the launch traced here: 314 us
  waiting for transfers between devices  110 us (35%)
  blocking collectives  89.2 us (28%)
  local copies, waits for them, and re-layouts  67.1 us (21%)
  other arithmetic  23.3 us (7%)
  between operations  16.3 us (5%)
  matrix products  6.54 us (2%)
    psum x1, waiting for transfers between devices, body(): lax.psum(weight_term, ('row', 'col', 'rep')) * float(node_total) ** (-0.5)  85.3 us
    all_gather x1, blocking collectives, body(): lax.all_gather(back, ('col', 'rep'), axis=0, tiled=True)  73.1 us
    gather x14, local copies, waits for them, and re-layouts, locate(): jnp.take(tile_vals, place, axis=0)  30.3 us
    reduce_scatter x1, waiting for transfers between devices, body(): lax.psum_scatter(dest_part.reshape(row_blocks * BLOCK, FEAT), ('col', 're...  25 us
    all_gather x1, blocking collectives, body(): gathered = lax.all_gather(feats, ('row', 'rep'), axis=0, tiled=True)  16.1 us
    gather x14, local copies, waits for them, and re-layouts, locate(): jnp.take(tile_cols, place)  13.6 us
    gather x14, local copies, waits for them, and re-layouts, locate(): jnp.take(tile_rows, place)  13.5 us
  transfers between devices with their start and end apart: 3, of which 2 were waited for; matrix products, arithmetic and copies ran while one was open for 14% of the time, Pallas kernels for 0%

commit v1 on v0

--- a/solution.py
+++ b/solution.py
@@ -1,10 +1,319 @@
+import functools
+
 import jax
 import jax.numpy as jnp
 from jax import lax
+from jax.experimental import pallas as pl
+from jax.experimental.pallas import tpu as pltpu
 from jax.sharding import PartitionSpec as P
 
 FEAT = 128
 BLOCK = 128
+LANES = 128
+SUBROWS = 16
+
+
+def fused(
+    rows_n, cols_n, reps_n, scale,
+    feats, weight, tiles, tile_rows, tile_cols, count, mask, cot,
+    act_o, gw_o, gx_o,
+    wv, tv, mv, cv, rv, kv, idx_v, idx_s, chain, a_send, a_recv, a_mat,
+    f_buf, b_buf, agg_s, agg_r, gx_s, gx_r, gw_s, gw_r, gw_b,
+    loc, idx_sem, fs, fr, bs, br, as_, ar, gs, gr, xs, xr, ws1, wr1, ws2, wr2,
+):
+    part = lax.axis_index("parts")
+    r = lax.axis_index("row")
+    c = lax.axis_index("col")
+    p = lax.axis_index("rep")
+    plane = cols_n * reps_n
+    total = rows_n * plane
+    chips = rows_n * cols_n
+    q = c * reps_n + p
+    me = r * plane + q
+    chip = r * cols_n + c
+    slots = tiles.shape[0]
+    row_blocks = plane
+    col_blocks = rows_n * reps_n
+
+    def at(flat):
+        return (part, flat // plane, (flat // reps_n) % cols_n, flat % reps_n)
+
+    def remote(src, dst, send, recv, device):
+        return pltpu.make_async_remote_copy(
+            src_ref=src, dst_ref=dst, send_sem=send, recv_sem=recv,
+            device_id=device, device_id_type=pl.DeviceIdType.MESH,
+        )
+
+    barrier = pltpu.get_barrier_semaphore()
+
+    @pl.loop(1, total)
+    def _(k):
+        pl.semaphore_signal(
+            barrier, inc=1, device_id=at(lax.rem(me + k, total)),
+            device_id_type=pl.DeviceIdType.MESH,
+        )
+
+    own_feats = f_buf.at[pl.ds(pl.multiple_of(r * BLOCK, BLOCK), BLOCK)]
+    loads = [
+        pltpu.make_async_copy(src, dst, loc.at[i])
+        for i, (src, dst) in enumerate(
+            [(tile_rows, rv), (tile_cols, kv), (mask, mv), (cot, cv), (weight, wv),
+             (feats, own_feats), (tiles, tv)]
+        )
+    ]
+    for copy in loads:
+        copy.start()
+
+    loads[0].wait()
+    loads[1].wait()
+    key = rv[...] * col_blocks + kv[...]
+    shape = (slots, LANES)
+    lane = lax.broadcasted_iota(jnp.int32, shape, 1)
+    sub = lax.broadcasted_iota(jnp.int32, shape, 0)
+    wide = jnp.concatenate([key, jnp.full((1, LANES - slots), -1, jnp.int32)], axis=1)
+    wide = jnp.broadcast_to(wide, shape)
+    tall = jnp.sum(jnp.where(lane == sub, wide, 0), axis=1, keepdims=True)
+    prev = jnp.where((tall == wide) & (sub < lane), sub + 1, 0)
+    last = jnp.where((tall == lane) & (sub < count[0]), sub + 1, 0)
+    idx_v[...] = jnp.zeros_like(idx_v)
+    idx_v[0:1, :] = jnp.max(prev, axis=0, keepdims=True)
+    idx_v[1:2, :] = jnp.max(last, axis=0, keepdims=True)
+    idx_copy = pltpu.make_async_copy(idx_v, idx_s, idx_sem)
+    idx_copy.start()
+
+    for copy in loads[2:6]:
+        copy.wait()
+    keep = mv[...].astype(jnp.float32)
+    grad_h = (cv[...].astype(jnp.float32) * keep).astype(jnp.bfloat16)
+    b_buf[q] = lax.dot_general(
+        wv[...], grad_h, (((1,), (1,)), ((), ())), preferred_element_type=jnp.float32
+    ).astype(jnp.bfloat16)
+
+    pl.semaphore_wait(barrier, total - 1)
+
+    f_copies = []
+    for k in range(1, rows_n):
+        copy = remote(
+            own_feats, own_feats, fs.at[k], fr.at[k],
+            (part, lax.rem(r + k, rows_n), c, p),
+        )
+        copy.start()
+        f_copies.append(copy)
+    b_copies = []
+    for k in range(1, plane):
+        other = lax.rem(q + k, plane)
+        copy = remote(
+            b_buf.at[q], b_buf.at[q], bs.at[k], br.at[k],
+            (part, r, other // reps_n, other % reps_n),
+        )
+        copy.start()
+        b_copies.append(copy)
+
+    loads[6].wait()
+    idx_copy.wait()
+    chain[0] = jnp.zeros((BLOCK, BLOCK), jnp.float32)
+
+    @pl.loop(0, slots)
+    def _(t):
+        chain[t + 1] = chain[idx_s[0, t]] + tv[t].astype(jnp.float32)
+
+    chunk = reps_n * BLOCK
+    a_copies = []
+    for k in range(cols_n):
+        dest = lax.rem(c + 1 + k, cols_n)
+        for j in range(reps_n):
+            for i in range(rows_n):
+                cell = (dest * reps_n + j) * col_blocks + i * reps_n + (1 - p)
+                a_send[k, pl.ds(j * BLOCK, BLOCK), pl.ds(i * BLOCK, BLOCK)] = chain[
+                    idx_s[1, cell]
+                ].astype(jnp.bfloat16)
+        copy = remote(a_send.at[k], a_recv.at[k], as_.at[k], ar.at[k], (part, r, c, 1 - p))
+        copy.start()
+        a_copies.append(copy)
+
+    for copy in f_copies:
+        copy.wait_recv()
+    g_copies = []
+    for k in range(cols_n):
+        dest = lax.rem(c + 1 + k, cols_n)
+        a_copies[k].wait_recv()
+        for j in range(reps_n):
+            for i in range(rows_n):
+                cell = (dest * reps_n + j) * col_blocks + i * reps_n + p
+                spot = (pl.ds(j * BLOCK, BLOCK), pl.ds(i * BLOCK, BLOCK))
+                a_mat[(k, *spot)] = (
+                    chain[idx_s[1, cell]] + a_recv[(k, *spot)].astype(jnp.float32)
+                ).astype(jnp.bfloat16)
+        partial = jnp.dot(
+            a_mat[k], f_buf[...], preferred_element_type=jnp.float32
+        ).astype(jnp.bfloat16)
+        for j in range(reps_n):
+            agg_s[k * reps_n + j] = partial[j * BLOCK:(j + 1) * BLOCK]
+        targets = range(reps_n) if k < cols_n - 1 else [1 - p]
+        for j in targets:
+            copy = remote(
+                agg_s.at[k * reps_n + j], agg_r.at[q], gs.at[k * reps_n + j], gr.at[q],
+                (part, r, dest, j),
+            )
+            copy.start()
+            g_copies.append(copy)
+
+    for copy in b_copies:
+        copy.wait_recv()
+    grad_t = jnp.zeros((FEAT, rows_n * BLOCK), jnp.float32)
+    for k in range(cols_n):
+        dest = lax.rem(c + 1 + k, cols_n)
+        pair = jnp.concatenate([b_buf[dest * reps_n + j] for j in range(reps_n)], axis=1)
+        grad_t += jnp.dot(pair, a_mat[k], preferred_element_type=jnp.float32)
+    for i in range(rows_n):
+        gx_s[i] = grad_t[:, i * BLOCK:(i + 1) * BLOCK].astype(jnp.bfloat16)
+    x_copies = []
+    for k in range(1, rows_n):
+        other = lax.rem(r + k, rows_n)
+        copy = remote(gx_s.at[other], gx_r.at[k], xs.at[k], xr.at[k], (part, other, c, p))
+        copy.start()
+        x_copies.append(copy)
+
+    agg = agg_s[(cols_n - 1) * reps_n + p].astype(jnp.float32)
+    for k in range(1, plane):
+        other = lax.rem(q + k, plane)
+        remote(agg_s.at[0], agg_r.at[other], gs.at[0], gr.at[other], (part, r, c, 1 - p)).wait_recv()
+        agg += agg_r[other].astype(jnp.float32)
+    agg_b = agg.astype(jnp.bfloat16)
+    term = lax.dot_general(
+        agg_b, grad_h, (((0,), (0,)), ((), ())), preferred_element_type=jnp.float32
+    ).astype(jnp.bfloat16)
+    per_half = FEAT // SUBROWS
+    for s in range(chips):
+        lo, half = (s % per_half) * SUBROWS, (s // per_half) * LANES
+        gw_s[s] = term[lo:lo + SUBROWS, half:half + LANES]
+
+    @pl.loop(1, chips)
+    def _(k):
+        other = lax.rem(chip + k, chips)
+        remote(
+            gw_s.at[other], gw_r.at[me], ws1, wr1, (part, other // cols_n, other % cols_n, 0)
+        ).start()
+
+    @pl.when(p != 0)
+    def _():
+        remote(gw_s.at[chip], gw_r.at[me], ws1, wr1, (part, r, c, 0)).start()
+
+    hidden = jnp.dot(agg_b, wv[...], preferred_element_type=jnp.float32)
+    act_o[...] = (hidden * keep).astype(jnp.bfloat16)
+
+    grad_t = gx_s[r].astype(jnp.float32)
+    for k, copy in enumerate(x_copies):
+        copy.wait_recv()
+        grad_t += gx_r[k + 1].astype(jnp.float32)
+    gx_o[...] = grad_t.T.astype(jnp.bfloat16)
+
+    @pl.when(p == 0)
+    def _():
+        gw_r[me] = gw_s[chip]
+        rest = gw_r.at[pl.ds(0, total - 1)]
+        remote(rest, rest, ws1, wr1, (part, r, c, 1 - p)).wait_recv()
+        terms = jnp.sum(gw_r[...].astype(jnp.float32), axis=0)
+        gw_b[chip] = (terms * scale).astype(jnp.bfloat16)
+
+        @pl.loop(1, total)
+        def _(k):
+            remote(gw_b.at[chip], gw_b.at[chip], ws2, wr2, at(lax.rem(me + k, total))).start()
+
+        rest = gw_b.at[pl.ds(0, chips - 1)]
+        remote(rest, rest, ws2, wr2, (part, r, c, 1 - p)).wait_recv()
+        sent = gw_r.at[pl.ds(0, total - 1)]
+        remote(sent, sent, ws2, wr2, (part, r, c, 1 - p)).wait_send()
+        sent = gw_s.at[pl.ds(0, chips - 1)]
+        remote(sent, sent, ws1, wr1, (part, r, c, 1 - p)).wait_send()
+
+    @pl.when(p != 0)
+    def _():
+        remote(gw_b, gw_b, ws2, wr2, (part, r, c, 0)).wait_recv()
+        remote(gw_s, gw_s, ws1, wr1, (part, r, c, 0)).wait_send()
+
+    for s in range(chips):
+        lo, half = (s % per_half) * SUBROWS, (s // per_half) * LANES
+        gw_o[lo:lo + SUBROWS, half:half + LANES] = gw_b[s].astype(jnp.float32)
+
+    for copy in f_copies + b_copies + a_copies + g_copies + x_copies:
+        copy.wait_send()
+
+
+def fused_body(rows_n, cols_n, reps_n, *args):
+    feats, weight, tiles, tile_rows, tile_cols, count, mask, cot = args
+    slots = tiles.shape[0]
+    hid = weight.shape[1]
+    plane = cols_n * reps_n
+    total = rows_n * plane
+    chips = rows_n * cols_n
+    nodes = feats.shape[0] * total
+    half = rows_n * BLOCK
+    b16, f32, i32 = jnp.bfloat16, jnp.float32, jnp.int32
+    dma = pltpu.SemaphoreType.DMA
+    anywhere = pl.BlockSpec(memory_space=pl.ANY)
+    vmem = pl.BlockSpec(memory_space=pltpu.VMEM)
+    return tuple(pl.pallas_call(
+        functools.partial(fused, rows_n, cols_n, reps_n, float(nodes) ** -0.5),
+        out_shape=(
+            jax.ShapeDtypeStruct((BLOCK, hid), b16),
+            jax.ShapeDtypeStruct((FEAT, hid), f32),
+            jax.ShapeDtypeStruct((BLOCK, FEAT), b16),
+        ),
+        in_specs=[anywhere] * 5 + [pl.BlockSpec(memory_space=pltpu.SMEM)] + [anywhere] * 2,
+        out_specs=(vmem, vmem, vmem),
+        scratch_shapes=[
+            pltpu.VMEM((FEAT, hid), b16),
+            pltpu.VMEM((slots, BLOCK, BLOCK), b16),
+            pltpu.VMEM((BLOCK, hid), i32),
+            pltpu.VMEM((BLOCK, hid), b16),
+            pltpu.VMEM((1, slots), i32),
+            pltpu.VMEM((1, slots), i32),
+            pltpu.VMEM((8, LANES), i32),
+            pltpu.SMEM((8, LANES), i32),
+            pltpu.VMEM((slots + 1, BLOCK, BLOCK), f32),
+            pltpu.VMEM((cols_n, reps_n * BLOCK, half), b16),
+            pltpu.VMEM((cols_n, reps_n * BLOCK, half), b16),
+            pltpu.VMEM((cols_n, reps_n * BLOCK, half), b16),
+            pltpu.VMEM((half, FEAT), b16),
+            pltpu.VMEM((plane, FEAT, BLOCK), b16),
+            pltpu.VMEM((plane, BLOCK, FEAT), b16),
+            pltpu.VMEM((plane, BLOCK, FEAT), b16),
+            pltpu.VMEM((rows_n, FEAT, BLOCK), b16),
+            pltpu.VMEM((rows_n, FEAT, BLOCK), b16),
+            pltpu.VMEM((chips, SUBROWS, LANES), b16),
+            pltpu.VMEM((total, SUBROWS, LANES), b16),
+            pltpu.VMEM((chips, SUBROWS, LANES), b16),
+            dma((7,)), dma,
+            dma((rows_n,)), dma((rows_n,)),
+            dma((plane,)), dma((plane,)),
+            dma((cols_n,)), dma((cols_n,)),
+            dma((plane,)), dma((plane,)),
+            dma((rows_n,)), dma((rows_n,)),
+            dma, dma, dma, dma,
+        ],
+        compiler_params=pltpu.CompilerParams(
+            collective_id=0, has_side_effects=True, vmem_limit_bytes=40 * 1024 * 1024
+        ),
+    )(
+        feats, weight, tiles, tile_rows.reshape(1, slots), tile_cols.reshape(1, slots),
+        count, mask, cot,
+    ))
+
+
+def fits(mesh, args):
+    rows_n, cols_n, reps_n = (mesh.shape[name] for name in ("row", "col", "rep"))
+    total = rows_n * cols_n * reps_n
+    hid = args[1].shape[1]
+    per_chip = SUBROWS * LANES * rows_n * cols_n
+    cells = rows_n * reps_n * cols_n * reps_n
+    return (
+        reps_n == 2
+        and cells <= LANES
+        and args[2].shape[0] // (total * mesh.shape["parts"]) <= LANES // 2
+        and args[0].shape[0] == total * BLOCK * mesh.shape["parts"]
+        and FEAT * hid == per_chip
+    )
 
 
 tiles_per_turn = 4
@@ -90,24 +399,21 @@
 
 
 def solution(mesh):
+    sizes = tuple(mesh.shape[name] for name in ("row", "col", "rep"))
+    spread = ("parts", "row", "col", "rep")
     placed = (
-        P(("parts", "row", "col", "rep"), None),
-        P(),
-        P(("parts", "row", "col", "rep"), None, None),
-        P(("parts", "row", "col", "rep")),
-        P(("parts", "row", "col", "rep")),
-        P(("parts", "row", "col", "rep")),
-        P(("parts", "row", "col", "rep"), None),
-        P(("parts", "row", "col", "rep"), None),
-    )
-    return jax.shard_map(
-        body,
-        mesh=mesh,
-        in_specs=placed,
-        out_specs=(
-            P(("parts", "row", "col", "rep"), None),
-            P("parts", None),
-            P(("parts", "row", "col", "rep"), None),
-        ),
-        check_vma=False,
-    )
+        P(spread, None), P(), P(spread, None, None), P(spread), P(spread), P(spread),
+        P(spread, None), P(spread, None),
+    )
+
+    def whole(*args):
+        local = functools.partial(fused_body, *sizes) if fits(mesh, args) else body
+        return jax.shard_map(
+            local,
+            mesh=mesh,
+            in_specs=placed,
+            out_specs=(P(spread, None), P("parts", None), P(spread, None)),
+            check_vma=False,
+        )(*args)
+
+    return whole

time: 315 us -> 35.4 us (0.11)
  waiting for transfers between devices: 110 us -> 0 us
  blocking collectives: 89.2 us -> 0 us
  local copies, waits for them, and re-layouts: 67.1 us -> 8.13 us
  Pallas kernels: 0 us -> 25.6 us
  other arithmetic: 23.3 us -> 0 us
  between operations: 16.3 us -> 1.3 us
  matrix products: 6.54 us -> 0 us
    all_gather x2 -> x0, blocking collectives: 89.2 us -> none  [the longest x1 73.1 us: body(): lax.all_gather(back, ('col', 'rep'), axis=0, tiled=True)]
    psum x1 -> x0, waiting for transfers between devices: 85.3 us -> none  [body(): lax.psum(weight_term, ('row', 'col', 'rep')) * float(node_total) ** (-0.5)]
    gather x56 -> x0, local copies, waits for them, and re-layouts: 65.5 us -> none  [the longest x14 30.3 us: locate(): jnp.take(tile_vals, place, axis=0)]
    pallas_call x0 -> x1, Pallas kernels: none -> 25.6 us  [fused_body(): pl.pallas_call(functools.partial(fused, rows_n, cols_n, reps_n, float(nod...]
    reduce_scatter x2 -> x0, waiting for transfers between devices: 25 us -> none  [the longest x1 25 us: body(): lax.psum_scatter(dest_part.reshape(row_blocks * BLOCK, FEAT), ('col', 're...]
    convert_element_type x15 -> x0, other arithmetic: 10.6 us -> none  [the longest x7 4.56 us: backward_step(): product = product * live.astype(jnp.float32)[:, None, None]]
    scatter-add x14 -> x0, other arithmetic: 10.5 us -> none  [the longest x7 5.26 us: backward_step(): return total.at[cols_here].add(product)]
    unnamed x16 -> x17, local copies, waits for them, and re-layouts: 1.59 us -> 8.13 us
  transfers between devices with their start and end apart: 3 -> 0, of which waited for: 2 -> 0; matrix products, arithmetic and copies ran while one was open for 14% -> 0% of each run, Pallas kernels for 0% -> 0%
where the time goes in v1:
time: 35.4 us; the launch traced here: 35.1 us
  Pallas kernels  25.6 us (72%)
  local copies, waits for them, and re-layouts  8.13 us (23%)
  between operations  1.3 us (4%)
    pallas_call x1, Pallas kernels, fused_body(): pl.pallas_call(functools.partial(fused, rows_n, cols_n, reps_n, float(nod...  25.6 us
    unnamed x17, local copies, waits for them, and re-layouts  8.13 us

profile of v1, /device:TPU:0, one launch (start us, length us, event | category | flops | bytes accessed | tf_op | source)
XLA Modules:
  0.0 35.1 jit_solution(18209904728926452678)
XLA Ops:
  1.3 0.0 copy-start
  1.3 1.6 %copy-done = bf16[64,128,128]{2,1,0:T(8,128)(2,1)S(1)} copy-done((bf16[64,128,128]{2,1,0:T(8,128)(2,1)S(1)}, bf16[64,128,128]{2,1,0:T(8,128)(2,1)}, u32[]{:S(2)}) %copy-start) | copy-done | bytes 2097176
  2.9 0.0 copy-start.1
  2.9 0.9 %copy-done.1 = s32[128,256]{1,0:T(8,128)S(1)} copy-done((s32[128,256]{1,0:T(8,128)S(1)}, s32[128,256]{1,0:T(8,128)}, u32[]{:S(2)}) %copy-start.1) | copy-done | bytes 131096
  3.8 0.0 copy-start.2
  3.8 0.8 %copy-done.2 = bf16[128,256]{1,0:T(8,128)(2,1)S(1)} copy-done((bf16[128,256]{1,0:T(8,128)(2,1)S(1)}, bf16[128,256]{1,0:T(8,128)(2,1)}, u32[]{:S(2)}) %copy-start.2) | copy-done | bytes 65560
  4.6 0.0 copy-start.3
  4.6 0.8 %copy-done.3 = bf16[128,256]{1,0:T(8,128)(2,1)S(1)} copy-done((bf16[128,256]{1,0:T(8,128)(2,1)S(1)}, bf16[128,256]{1,0:T(8,128)(2,1)}, u32[]{:S(2)}) %copy-start.3) | copy-done | bytes 65560
  5.5 0.0 copy-start.4
  5.5 0.8 %copy-done.4 = bf16[128,128]{1,0:T(8,128)(2,1)S(1)} copy-done((bf16[128,128]{1,0:T(8,128)(2,1)S(1)}, bf16[128,128]{1,0:T(8,128)(2,1)}, u32[]{:S(2)}) %copy-start.4) | copy-done | bytes 32792
  6.2 0.0 copy-start.5
  6.2 0.7 %copy-done.5 = s32[64]{0:T(128)S(1)} copy-done((s32[64]{0:T(128)S(1)}, s32[64]{0:T(128)}, u32[]{:S(2)}) %copy-start.5) | copy-done | bytes 280
  6.9 0.0 copy-start.6
  6.9 0.7 %copy-done.6 = s32[64]{0:T(128)S(1)} copy-done((s32[64]{0:T(128)S(1)}, s32[64]{0:T(128)}, u32[]{:S(2)}) %copy-start.6) | copy-done | bytes 280
  7.5 25.6 %shard_map.103 = (bf16[128,256]{1,0:T(8,128)(2,1)S(1)}, f32[128,256]{1,0:T(8,128)S(1)}, bf16[128,128]{1,0:T(8,128)(2,1)S(1)}) custom-call(bf16[128,128]{1,0:T(8,128)(2,1)S(1)} %copy-done.4, bf16[128,256]{1,0:T(8,128)(2,1)S(1)} %copy-done.2, bf16[64,128,128]{2,1,0:T(8,128)(2,1)S(1)} %copy-done, s32[1,64]{1,0:T(1,128)S(1)} %bitcast.2, s32[1,64]{1,0:T(1,128)S(1)} %bitcast.3, ...), custom_call_target="tpu_custom_call" | custom-call | tf_op jit(solution)/shard_map/pallas_call | solution.py:256
  33.2 0.6 %copy.15 = bf16[128,256]{1,0:T(8,128)(2,1)} copy(bf16[128,256]{1,0:T(8,128)(2,1)S(1)} %get-tuple-element.6) | data formatting | bytes 131072
  33.8 0.7 %copy.16 = f32[128,256]{1,0:T(8,128)} copy(f32[128,256]{1,0:T(8,128)S(1)} %get-tuple-element.7) | data formatting | bytes 262144
  34.4 0.6 %copy.17 = bf16[128,128]{1,0:T(8,128)(2,1)} copy(bf16[128,128]{1,0:T(8,128)(2,1)S(1)} %get-tuple-element.8) | data formatting | bytes 65536
Async XLA Ops:
  1.3 1.6 %copy-start = (bf16[64,128,128]{2,1,0:T(8,128)(2,1)S(1)}, bf16[64,128,128]{2,1,0:T(8,128)(2,1)}, u32[]{:S(2)}) copy-start(bf16[64,128,128]{2,1,0:T(8,128)(2,1)} %tiles.1) | copy-start | bytes 6291460
  2.9 0.9 %copy-start.1 = (s32[128,256]{1,0:T(8,128)S(1)}, s32[128,256]{1,0:T(8,128)}, u32[]{:S(2)}) copy-start(s32[128,256]{1,0:T(8,128)} %mask.1) | copy-start | bytes 393220
  3.8 0.8 %copy-start.2 = (bf16[128,256]{1,0:T(8,128)(2,1)S(1)}, bf16[128,256]{1,0:T(8,128)(2,1)}, u32[]{:S(2)}) copy-start(bf16[128,256]{1,0:T(8,128)(2,1)} %weight.1) | copy-start | bytes 196612
  4.6 0.8 %copy-start.3 = (bf16[128,256]{1,0:T(8,128)(2,1)S(1)}, bf16[128,256]{1,0:T(8,128)(2,1)}, u32[]{:S(2)}) copy-start(bf16[128,256]{1,0:T(8,128)(2,1)} %cot.1) | copy-start | bytes 196612
  5.5 0.8 %copy-start.4 = (bf16[128,128]{1,0:T(8,128)(2,1)S(1)}, bf16[128,128]{1,0:T(8,128)(2,1)}, u32[]{:S(2)}) copy-start(bf16[128,128]{1,0:T(8,128)(2,1)} %feats.1) | copy-start | bytes 98308
  6.2 0.7 %copy-start.5 = (s32[64]{0:T(128)S(1)}, s32[64]{0:T(128)}, u32[]{:S(2)}) copy-start(s32[64]{0:T(128)} %param.11) | copy-start | bytes 772
  6.9 0.7 %copy-start.6 = (s32[64]{0:T(128)S(1)}, s32[64]{0:T(128)}, u32[]{:S(2)}) copy-start(s32[64]{0:T(128)} %param.12) | copy-start | bytes 772

commit v2 on v1

--- a/solution.py
+++ b/solution.py
@@ -11,6 +11,7 @@
 BLOCK = 128
 LANES = 128
 SUBROWS = 16
+VMEM_LIMIT = 60 * 1024 * 1024
 
 
 def fused(
@@ -18,25 +19,18 @@
     feats, weight, tiles, tile_rows, tile_cols, count, mask, cot,
     act_o, gw_o, gx_o,
     wv, tv, mv, cv, rv, kv, idx_v, idx_s, chain, a_send, a_recv, a_mat,
-    f_buf, b_buf, agg_s, agg_r, gx_s, gx_r, gw_s, gw_r, gw_b,
-    loc, idx_sem, fs, fr, bs, br, as_, ar, gs, gr, xs, xr, ws1, wr1, ws2, wr2,
+    f_buf, b_buf, agg_s, agg_r, gx_s, gx_r, gw_s, gw_r, gw_z, gw_b, act_v, gx_v,
+    loc, idx_sem, fs, fr, bs, br, as_, ar, gs, gr, xs, xr, ws1, wr1, ws2, wr2, ws3, wr3,
 ):
     part = lax.axis_index("parts")
     r = lax.axis_index("row")
     c = lax.axis_index("col")
     p = lax.axis_index("rep")
     plane = cols_n * reps_n
-    total = rows_n * plane
-    chips = rows_n * cols_n
     q = c * reps_n + p
-    me = r * plane + q
-    chip = r * cols_n + c
     slots = tiles.shape[0]
     row_blocks = plane
     col_blocks = rows_n * reps_n
-
-    def at(flat):
-        return (part, flat // plane, (flat // reps_n) % cols_n, flat % reps_n)
 
     def remote(src, dst, send, recv, device):
         return pltpu.make_async_remote_copy(
@@ -46,11 +40,21 @@
 
     barrier = pltpu.get_barrier_semaphore()
 
-    @pl.loop(1, total)
-    def _(k):
+    def plane_peer(k):
+        other = lax.rem(q + k, plane)
+        return other, (part, r, other // reps_n, other % reps_n)
+
+    def row_peer(k):
+        other = lax.rem(r + k, rows_n)
+        return other, (part, other, c, p)
+
+    for k in range(1, plane):
         pl.semaphore_signal(
-            barrier, inc=1, device_id=at(lax.rem(me + k, total)),
-            device_id_type=pl.DeviceIdType.MESH,
+            barrier, inc=1, device_id=plane_peer(k)[1], device_id_type=pl.DeviceIdType.MESH
+        )
+    for k in range(1, rows_n):
+        pl.semaphore_signal(
+            barrier, inc=1, device_id=row_peer(k)[1], device_id_type=pl.DeviceIdType.MESH
         )
 
     own_feats = f_buf.at[pl.ds(pl.multiple_of(r * BLOCK, BLOCK), BLOCK)]
@@ -89,7 +93,7 @@
         wv[...], grad_h, (((1,), (1,)), ((), ())), preferred_element_type=jnp.float32
     ).astype(jnp.bfloat16)
 
-    pl.semaphore_wait(barrier, total - 1)
+    pl.semaphore_wait(barrier, plane + rows_n - 2)
 
     f_copies = []
     for k in range(1, rows_n):
@@ -183,61 +187,84 @@
     term = lax.dot_general(
         agg_b, grad_h, (((0,), (0,)), ((), ())), preferred_element_type=jnp.float32
     ).astype(jnp.bfloat16)
-    per_half = FEAT // SUBROWS
-    for s in range(chips):
-        lo, half = (s % per_half) * SUBROWS, (s // per_half) * LANES
-        gw_s[s] = term[lo:lo + SUBROWS, half:half + LANES]
-
-    @pl.loop(1, chips)
-    def _(k):
-        other = lax.rem(chip + k, chips)
-        remote(
-            gw_s.at[other], gw_r.at[me], ws1, wr1, (part, other // cols_n, other % cols_n, 0)
-        ).start()
-
-    @pl.when(p != 0)
-    def _():
-        remote(gw_s.at[chip], gw_r.at[me], ws1, wr1, (part, r, c, 0)).start()
+    piece = FEAT // plane
+    for i in range(plane):
+        gw_s[i] = term[i * piece:(i + 1) * piece]
+    w_copies = []
+    for k in range(1, plane):
+        other, device = plane_peer(k)
+        copy = remote(gw_s.at[other], gw_r.at[k], ws1.at[k], wr1.at[k], device)
+        copy.start()
+        w_copies.append(copy)
 
     hidden = jnp.dot(agg_b, wv[...], preferred_element_type=jnp.float32)
-    act_o[...] = (hidden * keep).astype(jnp.bfloat16)
+    act_v[...] = (hidden * keep).astype(jnp.bfloat16)
+    stores = [
+        pltpu.make_async_copy(act_v, act_o, loc.at[0]),
+        pltpu.make_async_copy(gx_v, gx_o, loc.at[1]),
+    ]
+    stores[0].start()
+
+    slab = gw_s[q].astype(jnp.float32)
+    for k in range(1, plane):
+        w_copies[k - 1].wait_recv()
+        slab += gw_r[k].astype(jnp.float32)
+    gw_z[r] = slab
+    z_copies = []
+    for k in range(1, rows_n):
+        copy = remote(gw_z.at[r], gw_z.at[r], ws2.at[k], wr2.at[k], row_peer(k)[1])
+        copy.start()
+        z_copies.append(copy)
+    for copy in z_copies:
+        copy.wait_recv()
+    gw_b[q] = (jnp.sum(gw_z[...], axis=0) * scale).astype(jnp.bfloat16)
+    o_copies = []
+    for k in range(1, plane):
+        copy = remote(gw_b.at[q], gw_b.at[q], ws3.at[k], wr3.at[k], plane_peer(k)[1])
+        copy.start()
+        o_copies.append(copy)
 
     grad_t = gx_s[r].astype(jnp.float32)
     for k, copy in enumerate(x_copies):
         copy.wait_recv()
         grad_t += gx_r[k + 1].astype(jnp.float32)
-    gx_o[...] = grad_t.T.astype(jnp.bfloat16)
-
-    @pl.when(p == 0)
-    def _():
-        gw_r[me] = gw_s[chip]
-        rest = gw_r.at[pl.ds(0, total - 1)]
-        remote(rest, rest, ws1, wr1, (part, r, c, 1 - p)).wait_recv()
-        terms = jnp.sum(gw_r[...].astype(jnp.float32), axis=0)
-        gw_b[chip] = (terms * scale).astype(jnp.bfloat16)
-
-        @pl.loop(1, total)
-        def _(k):
-            remote(gw_b.at[chip], gw_b.at[chip], ws2, wr2, at(lax.rem(me + k, total))).start()
-
-        rest = gw_b.at[pl.ds(0, chips - 1)]
-        remote(rest, rest, ws2, wr2, (part, r, c, 1 - p)).wait_recv()
-        sent = gw_r.at[pl.ds(0, total - 1)]
-        remote(sent, sent, ws2, wr2, (part, r, c, 1 - p)).wait_send()
-        sent = gw_s.at[pl.ds(0, chips - 1)]
-        remote(sent, sent, ws1, wr1, (part, r, c, 1 - p)).wait_send()
-
-    @pl.when(p != 0)
-    def _():
-        remote(gw_b, gw_b, ws2, wr2, (part, r, c, 0)).wait_recv()
-        remote(gw_s, gw_s, ws1, wr1, (part, r, c, 0)).wait_send()
-
-    for s in range(chips):
-        lo, half = (s % per_half) * SUBROWS, (s // per_half) * LANES
-        gw_o[lo:lo + SUBROWS, half:half + LANES] = gw_b[s].astype(jnp.float32)
-
+    gx_v[...] = grad_t.T.astype(jnp.bfloat16)
+    stores[1].start()
+
+    for copy in o_copies:
+        copy.wait_recv()
+    stores.append(pltpu.make_async_copy(gw_b, gw_o, loc.at[2]))
+    stores[2].start()
+
+    for copy in w_copies + z_copies + o_copies:
+        copy.wait_send()
+    for copy in stores:
+        copy.wait()
     for copy in f_copies + b_copies + a_copies + g_copies + x_copies:
         copy.wait_send()
+
+
+def hand_over(act, gw, gx, act_o, gw_o, gx_o, act_v, gw_v, gx_v, wide_v, sems):
+    loads = [
+        pltpu.make_async_copy(src, dst, sems.at[i])
+        for i, (src, dst) in enumerate([(gw, gw_v), (act, act_v), (gx, gx_v)])
+    ]
+    stores = [
+        pltpu.make_async_copy(src, dst, sems.at[3 + i])
+        for i, (src, dst) in enumerate([(wide_v, gw_o), (act_v, act_o), (gx_v, gx_o)])
+    ]
+    for copy in loads:
+        copy.start()
+    loads[0].wait()
+    piece = gw_v.shape[1]
+    for i in range(gw_v.shape[0]):
+        wide_v[i * piece:(i + 1) * piece, :] = gw_v[i].astype(jnp.float32)
+    stores[0].start()
+    for load, store in zip(loads[1:], stores[1:]):
+        load.wait()
+        store.start()
+    for copy in stores:
+        copy.wait()
 
 
 def fused_body(rows_n, cols_n, reps_n, *args):
@@ -246,22 +273,20 @@
     hid = weight.shape[1]
     plane = cols_n * reps_n
     total = rows_n * plane
-    chips = rows_n * cols_n
     nodes = feats.shape[0] * total
     half = rows_n * BLOCK
     b16, f32, i32 = jnp.bfloat16, jnp.float32, jnp.int32
     dma = pltpu.SemaphoreType.DMA
     anywhere = pl.BlockSpec(memory_space=pl.ANY)
-    vmem = pl.BlockSpec(memory_space=pltpu.VMEM)
-    return tuple(pl.pallas_call(
+    results = pl.pallas_call(
         functools.partial(fused, rows_n, cols_n, reps_n, float(nodes) ** -0.5),
         out_shape=(
             jax.ShapeDtypeStruct((BLOCK, hid), b16),
-            jax.ShapeDtypeStruct((FEAT, hid), f32),
+            jax.ShapeDtypeStruct((plane, FEAT // plane, hid), b16),
             jax.ShapeDtypeStruct((BLOCK, FEAT), b16),
         ),
         in_specs=[anywhere] * 5 + [pl.BlockSpec(memory_space=pltpu.SMEM)] + [anywhere] * 2,
-        out_specs=(vmem, vmem, vmem),
+        out_specs=(anywhere,) * 3,
         scratch_shapes=[
             pltpu.VMEM((FEAT, hid), b16),
             pltpu.VMEM((slots, BLOCK, BLOCK), b16),
@@ -281,38 +306,59 @@
             pltpu.VMEM((plane, BLOCK, FEAT), b16),
             pltpu.VMEM((rows_n, FEAT, BLOCK), b16),
             pltpu.VMEM((rows_n, FEAT, BLOCK), b16),
-            pltpu.VMEM((chips, SUBROWS, LANES), b16),
-            pltpu.VMEM((total, SUBROWS, LANES), b16),
-            pltpu.VMEM((chips, SUBROWS, LANES), b16),
+            pltpu.VMEM((plane, FEAT // plane, hid), b16),
+            pltpu.VMEM((plane, FEAT // plane, hid), b16),
+            pltpu.VMEM((rows_n, FEAT // plane, hid), f32),
+            pltpu.VMEM((plane, FEAT // plane, hid), b16),
+            pltpu.VMEM((BLOCK, hid), b16),
+            pltpu.VMEM((BLOCK, FEAT), b16),
             dma((7,)), dma,
             dma((rows_n,)), dma((rows_n,)),
             dma((plane,)), dma((plane,)),
             dma((cols_n,)), dma((cols_n,)),
             dma((plane,)), dma((plane,)),
             dma((rows_n,)), dma((rows_n,)),
-            dma, dma, dma, dma,
+            dma((plane,)), dma((plane,)),
+            dma((rows_n,)), dma((rows_n,)),
+            dma((plane,)), dma((plane,)),
         ],
         compiler_params=pltpu.CompilerParams(
-            collective_id=0, has_side_effects=True, vmem_limit_bytes=40 * 1024 * 1024
+            collective_id=0, has_side_effects=True, vmem_limit_bytes=VMEM_LIMIT
         ),
     )(
         feats, weight, tiles, tile_rows.reshape(1, slots), tile_cols.reshape(1, slots),
         count, mask, cot,
-    ))
+    )
+    return tuple(pl.pallas_call(
+        hand_over,
+        out_shape=(
+            jax.ShapeDtypeStruct((BLOCK, hid), b16),
+            jax.ShapeDtypeStruct((FEAT, hid), f32),
+            jax.ShapeDtypeStruct((BLOCK, FEAT), b16),
+        ),
+        in_specs=[anywhere] * 3,
+        out_specs=(anywhere,) * 3,
+        scratch_shapes=[
+            pltpu.VMEM((BLOCK, hid), b16),
+            pltpu.VMEM((plane, FEAT // plane, hid), b16),
+            pltpu.VMEM((BLOCK, FEAT), b16),
+            pltpu.VMEM((FEAT, hid), f32),
+            dma((6,)),
+        ],
+        compiler_params=pltpu.CompilerParams(vmem_limit_bytes=VMEM_LIMIT),
+    )(*results))
 
 
 def fits(mesh, args):
     rows_n, cols_n, reps_n = (mesh.shape[name] for name in ("row", "col", "rep"))
     total = rows_n * cols_n * reps_n
-    hid = args[1].shape[1]
-    per_chip = SUBROWS * LANES * rows_n * cols_n
     cells = rows_n * reps_n * cols_n * reps_n
     return (
         reps_n == 2
         and cells <= LANES
         and args[2].shape[0] // (total * mesh.shape["parts"]) <= LANES // 2
         and args[0].shape[0] == total * BLOCK * mesh.shape["parts"]
-        and FEAT * hid == per_chip
+        and FEAT % (SUBROWS * cols_n * reps_n) == 0
     )
 
 

time: 35.4 us -> 29.5 us (0.83)
  local copies, waits for them, and re-layouts: 8.13 us -> 0 us
  Pallas kernels: 25.6 us -> 28 us
    unnamed x17 -> x0, local copies, waits for them, and re-layouts: 8.13 us -> none
    pallas_call x0 -> x1, Pallas kernels: none -> 1.58 us  [fused_body(): pl.pallas_call(hand_over, out_shape=(jax.ShapeDtypeStruct((BLOCK, hid), b...]
    pallas_call x1, Pallas kernels: 25.6 us -> 26.4 us  [fused_body(): pl.pallas_call(functools.partial(fused, rows_n, cols_n, reps_n, float(nod...]
where the time goes in v2:
time: 29.5 us; the launch traced here: 29.3 us
  Pallas kernels  28 us (95%)
  between operations  1.29 us (4%)
    pallas_call x1, Pallas kernels, fused_body(): pl.pallas_call(functools.partial(fused, rows_n, cols_n, reps_n, float(nod...  26.4 us
    pallas_call x1, Pallas kernels, fused_body(): pl.pallas_call(hand_over, out_shape=(jax.ShapeDtypeStruct((BLOCK, hid), b...  1.58 us

profile of v2, /device:TPU:0, one launch (start us, length us, event | category | flops | bytes accessed | tf_op | source)
XLA Modules:
  0.0 29.3 jit_solution(4719875148718948854)
XLA Ops:
  1.3 26.4 %shard_map.103 = (bf16[128,256]{1,0:T(8,128)(2,1)}, bf16[8,16,256]{2,1,0:T(8,128)(2,1)}, bf16[128,128]{1,0:T(8,128)(2,1)}) custom-call(bf16[128,128]{1,0:T(8,128)(2,1)} %feats.1, bf16[128,256]{1,0:T(8,128)(2,1)} %weight.1, bf16[64,128,128]{2,1,0:T(8,128)(2,1)} %tiles.1, s32[1,64]{1,0:T(1,128)} %bitcast.2, s32[1,64]{1,0:T(1,128)} %bitcast.3, ...), custom_call_target="tpu_custom_call" | custom-call | tf_op jit(solution)/shard_map/pallas_call | solution.py:281
  27.7 1.6 %shard_map.104 = (bf16[128,256]{1,0:T(8,128)(2,1)}, f32[128,256]{1,0:T(8,128)}, bf16[128,128]{1,0:T(8,128)(2,1)}) custom-call(bf16[128,256]{1,0:T(8,128)(2,1)} %get-tuple-element.6.act, bf16[8,16,256]{2,1,0:T(8,128)(2,1)} %get-tuple-element.7.gw, bf16[128,128]{1,0:T(8,128)(2,1)} %get-tuple-element.8.gx), custom_call_target="tpu_custom_call" | custom-call | tf_op jit(solution)/shard_map/pallas_call | solution.py:332

commit v3 on v2

--- a/solution.py
+++ b/solution.py
@@ -65,8 +65,20 @@
              (feats, own_feats), (tiles, tv)]
         )
     ]
-    for copy in loads:
-        copy.start()
+    for copy in loads[5:6] + loads[:5] + loads[6:]:
+        copy.start()
+
+    loads[5].wait()
+    pl.semaphore_wait(barrier, plane + rows_n - 2)
+
+    f_copies = []
+    for k in range(1, rows_n):
+        copy = remote(
+            own_feats, own_feats, fs.at[k], fr.at[k],
+            (part, lax.rem(r + k, rows_n), c, p),
+        )
+        copy.start()
+        f_copies.append(copy)
 
     loads[0].wait()
     loads[1].wait()
@@ -85,7 +97,7 @@
     idx_copy = pltpu.make_async_copy(idx_v, idx_s, idx_sem)
     idx_copy.start()
 
-    for copy in loads[2:6]:
+    for copy in loads[2:5]:
         copy.wait()
     keep = mv[...].astype(jnp.float32)
     grad_h = (cv[...].astype(jnp.float32) * keep).astype(jnp.bfloat16)
@@ -93,16 +105,6 @@
         wv[...], grad_h, (((1,), (1,)), ((), ())), preferred_element_type=jnp.float32
     ).astype(jnp.bfloat16)
 
-    pl.semaphore_wait(barrier, plane + rows_n - 2)
-
-    f_copies = []
-    for k in range(1, rows_n):
-        copy = remote(
-            own_feats, own_feats, fs.at[k], fr.at[k],
-            (part, lax.rem(r + k, rows_n), c, p),
-        )
-        copy.start()
-        f_copies.append(copy)
     b_copies = []
     for k in range(1, plane):
         other = lax.rem(q + k, plane)
@@ -135,9 +137,6 @@
         copy.start()
         a_copies.append(copy)
 
-    for copy in f_copies:
-        copy.wait_recv()
-    g_copies = []
     for k in range(cols_n):
         dest = lax.rem(c + 1 + k, cols_n)
         a_copies[k].wait_recv()
@@ -148,6 +147,12 @@
                 a_mat[(k, *spot)] = (
                     chain[idx_s[1, cell]] + a_recv[(k, *spot)].astype(jnp.float32)
                 ).astype(jnp.bfloat16)
+
+    for copy in f_copies:
+        copy.wait_recv()
+    g_copies = []
+    for k in range(cols_n):
+        dest = lax.rem(c + 1 + k, cols_n)
         partial = jnp.dot(
             a_mat[k], f_buf[...], preferred_element_type=jnp.float32
         ).astype(jnp.bfloat16)

time: 29.5 us -> 29.3 us (level)
  no operation moved by 1% of the time
where the time goes in v3:
time: 29.3 us; the launch traced here: 29.1 us
  Pallas kernels  27.8 us (95%)
  between operations  1.29 us (4%)
    pallas_call x1, Pallas kernels, fused_body(): pl.pallas_call(functools.partial(fused, rows_n, cols_n, reps_n, float(nod...  26.2 us
    pallas_call x1, Pallas kernels, fused_body(): pl.pallas_call(hand_over, out_shape=(jax.ShapeDtypeStruct((BLOCK, hid), b...  1.58 us

profile of v3, /device:TPU:0, one launch (start us, length us, event | category | flops | bytes accessed | tf_op | source)
XLA Modules:
  0.0 29.1 jit_solution(10076238137237833408)
XLA Ops:
  1.3 26.2 %shard_map.103 = (bf16[128,256]{1,0:T(8,128)(2,1)}, bf16[8,16,256]{2,1,0:T(8,128)(2,1)}, bf16[128,128]{1,0:T(8,128)(2,1)}) custom-call(bf16[128,128]{1,0:T(8,128)(2,1)} %feats.1, bf16[128,256]{1,0:T(8,128)(2,1)} %weight.1, bf16[64,128,128]{2,1,0:T(8,128)(2,1)} %tiles.1, s32[1,64]{1,0:T(1,128)} %bitcast.2, s32[1,64]{1,0:T(1,128)} %bitcast.3, ...), custom_call_target="tpu_custom_call" | custom-call | tf_op jit(solution)/shard_map/pallas_call | solution.py:286
  27.5 1.6 %shard_map.104 = (bf16[128,256]{1,0:T(8,128)(2,1)}, f32[128,256]{1,0:T(8,128)}, bf16[128,128]{1,0:T(8,128)(2,1)}) custom-call(bf16[128,256]{1,0:T(8,128)(2,1)} %get-tuple-element.6.act, bf16[8,16,256]{2,1,0:T(8,128)(2,1)} %get-tuple-element.7.gw, bf16[128,128]{1,0:T(8,128)(2,1)} %get-tuple-element.8.gx), custom_call_target="tpu_custom_call" | custom-call | tf_op jit(solution)/shard_map/pallas_call | solution.py:337
